TPU v7x, 32 devices: a whole 2x2x4 slice. The times are simulated.
32 devices in a mesh: groups: 2 (over y), gx: 4 (over z), gy: 2 (over x), layer: 2 (over core).
Axes of the slice: x: 2, y: 2, z: 4, core: 2. Of those that a mesh axis runs over, the one named last changes fastest.
Arguments:
- density: bfloat16 [8, 6, 5, 184, 184], P(('groups', 'gx'), 'gy', None, 'layer'), parts along dimension 0
- pattern: int32 [8, 6, 5], P(('groups', 'gx'), 'gy'), parts along dimension 0, may hold values from 0 to 1, as said below
Outputs:
- purified: bfloat16 [8, 6, 5, 184, 184], P(('groups', 'gx'), 'gy', None, 'layer'), parts along dimension 0
There are 2 independent parts, one for each index of `groups`. A program takes and returns all parts, laid end to end along the dimension named above; each array names one. Nothing has to cross between parts.
Inputs may be any that keep to these rules, and one draw needn't show every extreme that they name: `pattern`: slot 0 is always 1; slot 1 of cluster (x, y) equals slot 2 of cluster (x + 1, y), and slot 3 equals slot 4 of cluster (x, y + 1).
All inputs are finite; a program needn't handle non-finite values.
Results may differ from a plain program's by a relative error of at most 0.012.
The roundings to bfloat16 on the way count: a program that leaves them out, or rounds other values in their place, can miss the bound.
Values may be sent and summed in bfloat16 or wider, within the bound.
A program may use at most 64 MiB of HBM per device.

v0:
```python
import jax
import jax.numpy as jnp
from jax import lax
from jax.sharding import PartitionSpec as P

STEPS = 2


OFFSETS = ((0, 0), (1, 0), (-1, 0), (0, 1), (0, -1))
PAIRS = (
    ((0, 0), (1, 2), (2, 1), (3, 4), (4, 3)),
    ((0, 1), (1, 0)),
    ((0, 2), (2, 0)),
    ((0, 3), (3, 0)),
    ((0, 4), (4, 0)),
)


def padded(block, sides, width):
    for axis, dim in sides:
        count = lax.axis_size(axis)
        forward = [(i, i + 1) for i in range(count - 1)]
        forward.append((count - 1, 0))
        backward = [(target, source) for source, target in forward]
        low = lax.ppermute(
            lax.slice_in_dim(block, block.shape[dim] - width, None, axis=dim), axis, forward
        )
        high = lax.ppermute(lax.slice_in_dim(block, 0, width, axis=dim), axis, backward)
        block = jnp.concatenate([low, block, high], axis=dim)
    return block


def truncated(left, extended, keep):
    count_x, count_y = (left.shape[0], left.shape[1])
    slots = []
    for pairs in PAIRS:
        total = jnp.zeros(left[:, :, 0].shape, jnp.float32)
        for first, second in pairs:
            shift_x, shift_y = OFFSETS[first]
            partner = extended[
                1 + shift_x : 1 + shift_x + count_x, 1 + shift_y : 1 + shift_y + count_y, second
            ]
            total = total + jnp.einsum(
                "xyij,xyjk->xyik", left[:, :, first], partner, preferred_element_type=jnp.float32
            )
        slots.append(total)
    return lax.optimization_barrier((jnp.stack(slots, 2) * keep).astype(jnp.bfloat16))


def border(source):
    return padded(source, (("gx", 0), ("gy", 1)), 1)


def on_device(density, pattern):
    keep = pattern[:, :, :, None, None].astype(jnp.float32)
    current = density * pattern[:, :, :, None, None].astype(jnp.bfloat16)
    for step in range(STEPS):
        joined = lax.all_gather(current, "layer", axis=3, tiled=True)
        extended = border(joined)
        square = truncated(current, extended, keep)
        cube = truncated(square, extended, keep)
        current = (3.0 * square.astype(jnp.float32) - 2.0 * cube.astype(jnp.float32)).astype(
            jnp.bfloat16
        )
    return current


def solution(mesh):
    return jax.shard_map(
        on_device,
        mesh=mesh,
        in_specs=(P(("groups", "gx"), "gy", None, "layer", None), P(("groups", "gx"), "gy", None)),
        out_specs=P(("groups", "gx"), "gy", None, "layer", None),
        check_vma=False,
    )
```

profile of v0, /device:TPU:0, one launch (start us, length us, event | category | flops | bytes accessed | tf_op | source)
XLA Modules:
  0.0 290.0 jit_solution(1140878483878854598)
XLA Ops:
  0.0 0.8 fusion.80
  0.9 1.3 copy_multiply_fusion
  2.2 1.1 copy.9
  3.3 3.4 %all_gather.6 = bf16[1,3,5,184,184]{4,1,2,0,3:T(4,128)(2,1)} all-gather(bf16[1,3,5,92,184]{4,1,2,0,3:T(4,128)(2,1)S(1)} %copy.9), channel_id=1, replica_groups=mesh['groups'=2,'gx'=4,'gy'=2,'layer'=2] {'layer'}, dimensions={3}, use_global_device_ids=true | all-gather | bytes 1523520 | tf_op jit(solution)/shard_map/all_gather | solution.py:58
  6.6 3.6 %copy.10 = bf16[1,3,5,184,184]{3,4,1,2,0:T(8,128)(2,1)S(1)} copy(bf16[1,3,5,184,184]{4,1,2,0,3:T(4,128)(2,1)} %all_gather.6) | data formatting | bytes 2031360 | tf_op jit(solution)/shard_map/all_gather | solution.py:58
  10.3 5.0 %collective-permute-start = (bf16[1,3,5,184,184]{3,4,1,2,0:T(8,128)(2,1)S(1)}, bf16[1,3,5,184,184]{3,4,1,2,0:T(8,128)(2,1)S(1)}, u32[]{:S(2)}, u32[]{:S(2)}) collective-permute-start(bf16[1,3,5,184,184]{3,4,1,2,0:T(8,128)(2,1)S(1)} %copy.10), channel_id=1, source_target_pairs={{4,0},{8,4},{12,8},{0,12},{5,1},{9,5},{13,9},{1,13},{6,2},{10,6},{... | collective-permute-start | bytes 3047048 | tf_op jit(solution)/shard_map/ppermute | solution.py:28
  15.3 0.9 fusion.53
  16.3 30.4 %collective-permute-done = bf16[1,3,5,184,184]{3,4,1,2,0:T(8,128)(2,1)S(1)} collective-permute-done((bf16[1,3,5,184,184]{3,4,1,2,0:T(8,128)(2,1)S(1)}, bf16[1,3,5,184,184]{3,4,1,2,0:T(8,128)(2,1)S(1)}, u32[]{:S(2)}, u32[]{:S(2)}) %collective-permute-start) | collective-permute-done | bytes 1015712 | tf_op jit(solution)/shard_map/ppermute | solution.py:28
  46.7 30.3 %collective-permute-done.1 = bf16[1,3,5,184,184]{3,4,1,2,0:T(8,128)(2,1)S(1)} collective-permute-done((bf16[1,3,5,184,184]{3,4,1,2,0:T(8,128)(2,1)S(1)}, bf16[1,3,5,184,184]{3,4,1,2,0:T(8,128)(2,1)S(1)}, u32[]{:S(2)}, u32[]{:S(2)}) %collective-permute-start.1) | collective-permute-done | bytes 1015712 | tf_op jit(solution)/shard_map/ppermute | solution.py:25
  77.0 2.2 pad_maximum_fusion.5
  79.3 1.5 collective-permute-start.3
  80.7 0.5 collective-permute-start.2
  81.3 0.9 fusion.55
  83.0 0.6 copy-done.1
  83.7 0.2 convolution_add_fusion.23
  83.9 29.5 %collective-permute-done.3 = bf16[3,1,5,184,184]{3,4,1,2,0:T(8,128)(2,1)} collective-permute-done((bf16[3,1,5,184,184]{3,4,1,2,0:T(8,128)(2,1)}, bf16[3,1,5,184,184]{3,4,1,2,0:T(8,128)(2,1)}, u32[]{:S(2)}, u32[]{:S(2)}) %collective-permute-start.3) | collective-permute-done | bytes 1015712 | tf_op jit(solution)/shard_map/ppermute | solution.py:25
  113.5 28.6 %collective-permute-done.2 = bf16[3,1,5,184,184]{3,4,1,2,0:T(8,128)(2,1)} collective-permute-done((bf16[3,1,5,184,184]{3,4,1,2,0:T(8,128)(2,1)}, bf16[3,1,5,184,184]{3,4,1,2,0:T(8,128)(2,1)}, u32[]{:S(2)}, u32[]{:S(2)}) %collective-permute-start.2) | collective-permute-done | bytes 1015712 | tf_op jit(solution)/shard_map/ppermute | solution.py:28
  142.0 1.3 fusion.50
  143.8 0.2 fusion.6
  144.0 0.2 copy-done.2
  144.3 0.2 fusion.17
  144.5 0.2 fusion.19
  144.7 0.2 fusion.21
  145.0 0.2 fusion.23
  145.4 0.2 fusion.75
  146.1 0.2 fusion.54
  146.4 0.2 fusion.56
  146.6 0.2 fusion.58
  147.3 0.2 fusion.9
  147.5 0.2 fusion.25
  147.8 0.2 fusion.27
  148.0 0.2 fusion.29
  148.7 0.3 subtract_convert_fusion.1
  149.0 1.1 copy.19
  150.1 3.3 %all_gather.7 = bf16[1,3,5,184,184]{4,1,2,0,3:T(4,128)(2,1)} all-gather(bf16[1,3,5,92,184]{4,1,2,0,3:T(4,128)(2,1)S(1)} %copy.19), channel_id=1, replica_groups=mesh['groups'=2,'gx'=4,'gy'=2,'layer'=2] {'layer'}, dimensions={3}, use_global_device_ids=true | all-gather | bytes 1523520 | tf_op jit(solution)/shard_map/all_gather | solution.py:58
  153.4 3.6 %copy.20 = bf16[1,3,5,184,184]{3,4,1,2,0:T(8,128)(2,1)S(1)} copy(bf16[1,3,5,184,184]{4,1,2,0,3:T(4,128)(2,1)} %all_gather.7) | data formatting | bytes 2031360 | tf_op jit(solution)/shard_map/all_gather | solution.py:58
  157.0 1.5 collective-permute-start.4
  158.5 0.6 collective-permute-start.5
  159.3 32.0 %collective-permute-done.4 = bf16[1,3,5,184,184]{3,4,1,2,0:T(8,128)(2,1)S(1)} collective-permute-done((bf16[1,3,5,184,184]{3,4,1,2,0:T(8,128)(2,1)S(1)}, bf16[1,3,5,184,184]{3,4,1,2,0:T(8,128)(2,1)S(1)}, u32[]{:S(2)}, u32[]{:S(2)}) %collective-permute-start.4) | collective-permute-done | bytes 1015712 | tf_op jit(solution)/shard_map/ppermute | solution.py:28
  191.3 29.0 %collective-permute-done.5 = bf16[1,3,5,184,184]{3,4,1,2,0:T(8,128)(2,1)S(1)} collective-permute-done((bf16[1,3,5,184,184]{3,4,1,2,0:T(8,128)(2,1)S(1)}, bf16[1,3,5,184,184]{3,4,1,2,0:T(8,128)(2,1)S(1)}, u32[]{:S(2)}, u32[]{:S(2)}) %collective-permute-start.5) | collective-permute-done | bytes 1015712 | tf_op jit(solution)/shard_map/ppermute | solution.py:25
  220.3 0.6 pad_maximum_fusion.2
  221.0 1.5 collective-permute-start.7
  222.5 0.5 collective-permute-start.6
  224.0 0.2 convolution_add_fusion.11
  224.2 30.7 %collective-permute-done.7 = bf16[3,1,5,184,184]{3,4,1,2,0:T(8,128)(2,1)S(1)} collective-permute-done((bf16[3,1,5,184,184]{3,4,1,2,0:T(8,128)(2,1)S(1)}, bf16[3,1,5,184,184]{3,4,1,2,0:T(8,128)(2,1)S(1)}, u32[]{:S(2)}, u32[]{:S(2)}) %collective-permute-start.7) | collective-permute-done | bytes 1015712 | tf_op jit(solution)/shard_map/ppermute | solution.py:25
  254.9 28.5 %collective-permute-done.6 = bf16[3,1,5,184,184]{3,4,1,2,0:T(8,128)(2,1)S(1)} collective-permute-done((bf16[3,1,5,184,184]{3,4,1,2,0:T(8,128)(2,1)S(1)}, bf16[3,1,5,184,184]{3,4,1,2,0:T(8,128)(2,1)S(1)}, u32[]{:S(2)}, u32[]{:S(2)}) %collective-permute-start.6) | collective-permute-done | bytes 1015712 | tf_op jit(solution)/shard_map/ppermute | solution.py:28
  283.4 0.2 fusion.48
  284.1 0.2 fusion.12
  284.4 0.2 fusion.33
  284.6 0.2 fusion.35
  284.8 0.2 fusion.37
  285.1 0.2 fusion.39
  286.2 0.2 fusion.64
  286.4 0.2 fusion.66
  286.7 0.2 fusion.68
  286.9 0.2 fusion.70
  287.1 0.2 convolution_add_fusion.5
  287.4 0.2 fusion.15
  287.6 0.2 fusion.41
  287.9 0.2 fusion.43
  288.1 0.2 fusion.45
  288.4 0.2 fusion.47
  288.8 0.3 subtract_convert_fusion
  289.1 0.9 copy.28
  (33 shorter events, 5.5 us)
Async XLA Ops:
  10.3 36.4 %collective-permute-start = (bf16[1,3,5,184,184]{3,4,1,2,0:T(8,128)(2,1)S(1)}, bf16[1,3,5,184,184]{3,4,1,2,0:T(8,128)(2,1)S(1)}, u32[]{:S(2)}, u32[]{:S(2)}) collective-permute-start(bf16[1,3,5,184,184]{3,4,1,2,0:T(8,128)(2,1)S(1)} %copy.10), channel_id=1, source_target_pairs={{4,0},{8,4},{12,8},{0,12},{5,1},{9,5},{13,9},{1,13},{6,2},{10,6},{... | collective-permute-start | bytes 3047048 | tf_op jit(solution)/shard_map/ppermute | solution.py:28
  15.3 61.7 %collective-permute-start.1 = (bf16[1,3,5,184,184]{3,4,1,2,0:T(8,128)(2,1)S(1)}, bf16[1,3,5,184,184]{3,4,1,2,0:T(8,128)(2,1)S(1)}, u32[]{:S(2)}, u32[]{:S(2)}) collective-permute-start(bf16[1,3,5,184,184]{3,4,1,2,0:T(8,128)(2,1)S(1)} %copy.10), channel_id=1, source_target_pairs={{0,4},{4,8},{8,12},{12,0},{1,5},{5,9},{9,13},{13,1},{2,6},{6,10},{... | collective-permute-start | bytes 3047048 | tf_op jit(solution)/shard_map/ppermute | solution.py:25
  46.7 32.6 %copy-start = (bf16[1,3,5,184,184]{3,4,1,2,0:T(8,128)(2,1)}, bf16[1,3,5,184,184]{3,4,1,2,0:T(8,128)(2,1)S(1)}, u32[]{:S(2)}) copy-start(bf16[1,3,5,184,184]{3,4,1,2,0:T(8,128)(2,1)S(1)} %collective-permute-done) | copy-start | bytes 3047044
  79.3 34.2 %collective-permute-start.3 = (bf16[3,1,5,184,184]{3,4,1,2,0:T(8,128)(2,1)}, bf16[3,1,5,184,184]{3,4,1,2,0:T(8,128)(2,1)}, u32[]{:S(2)}, u32[]{:S(2)}) collective-permute-start(bf16[3,1,5,184,184]{3,4,1,2,0:T(8,128)(2,1)} %get-tuple-element.20), channel_id=1, source_target_pairs={{0,2},{2,0},{1,3},{3,1},{4,6},{6,4},{5,7},{7,5},{8,10},{10,8},{9,1... | collective-permute-start | bytes 3047048 | tf_op jit(solution)/shard_map/ppermute | solution.py:25
  80.7 61.3 %collective-permute-start.2 = (bf16[3,1,5,184,184]{3,4,1,2,0:T(8,128)(2,1)}, bf16[3,1,5,184,184]{3,4,1,2,0:T(8,128)(2,1)}, u32[]{:S(2)}, u32[]{:S(2)}) collective-permute-start(bf16[3,1,5,184,184]{3,4,1,2,0:T(8,128)(2,1)} %get-tuple-element.19), channel_id=1, source_target_pairs={{2,0},{0,2},{3,1},{1,3},{6,4},{4,6},{7,5},{5,7},{10,8},{8,10},{11,... | collective-permute-start | bytes 3047048 | tf_op jit(solution)/shard_map/ppermute | solution.py:28
  82.3 1.4 copy-start.1
  82.3 1.4 copy-start.3
  143.3 1.0 copy-start.2
  157.0 34.3 %collective-permute-start.4 = (bf16[1,3,5,184,184]{3,4,1,2,0:T(8,128)(2,1)S(1)}, bf16[1,3,5,184,184]{3,4,1,2,0:T(8,128)(2,1)S(1)}, u32[]{:S(2)}, u32[]{:S(2)}) collective-permute-start(bf16[1,3,5,184,184]{3,4,1,2,0:T(8,128)(2,1)S(1)} %copy.20), channel_id=1, source_target_pairs={{4,0},{8,4},{12,8},{0,12},{5,1},{9,5},{13,9},{1,13},{6,2},{10,6},{... | collective-permute-start | bytes 3047048 | tf_op jit(solution)/shard_map/ppermute | solution.py:28
  158.5 61.9 %collective-permute-start.5 = (bf16[1,3,5,184,184]{3,4,1,2,0:T(8,128)(2,1)S(1)}, bf16[1,3,5,184,184]{3,4,1,2,0:T(8,128)(2,1)S(1)}, u32[]{:S(2)}, u32[]{:S(2)}) collective-permute-start(bf16[1,3,5,184,184]{3,4,1,2,0:T(8,128)(2,1)S(1)} %copy.20), channel_id=1, source_target_pairs={{0,4},{4,8},{8,12},{12,0},{1,5},{5,9},{9,13},{13,1},{2,6},{6,10},{... | collective-permute-start | bytes 3047048 | tf_op jit(solution)/shard_map/ppermute | solution.py:25
  221.0 34.0 %collective-permute-start.7 = (bf16[3,1,5,184,184]{3,4,1,2,0:T(8,128)(2,1)S(1)}, bf16[3,1,5,184,184]{3,4,1,2,0:T(8,128)(2,1)S(1)}, u32[]{:S(2)}, u32[]{:S(2)}) collective-permute-start(bf16[3,1,5,184,184]{3,4,1,2,0:T(8,128)(2,1)S(1)} %get-tuple-element.16), channel_id=1, source_target_pairs={{0,2},{2,0},{1,3},{3,1},{4,6},{6,4},{5,7},{7,5},{8,10},{10,8},{9,1... | collective-permute-start | bytes 3047048 | tf_op jit(solution)/shard_map/ppermute | solution.py:25
  222.5 60.9 %collective-permute-start.6 = (bf16[3,1,5,184,184]{3,4,1,2,0:T(8,128)(2,1)S(1)}, bf16[3,1,5,184,184]{3,4,1,2,0:T(8,128)(2,1)S(1)}, u32[]{:S(2)}, u32[]{:S(2)}) collective-permute-start(bf16[3,1,5,184,184]{3,4,1,2,0:T(8,128)(2,1)S(1)} %get-tuple-element.15), channel_id=1, source_target_pairs={{2,0},{0,2},{3,1},{1,3},{6,4},{4,6},{7,5},{5,7},{10,8},{8,10},{11,... | collective-permute-start | bytes 3047048 | tf_op jit(solution)/shard_map/ppermute | solution.py:28
where the time goes:
time: 290 us
  waiting for transfers between devices  239 us (82%)
  matrix products  13.4 us (5%)
  local copies, waits for them, and re-layouts  11.5 us (4%)
  starting transfers between devices  11.2 us (4%)
  other arithmetic  7.71 us (3%)
  blocking collectives  6.65 us (2%)
    ppermute x4, waiting for transfers between devices, padded(): lax.ppermute(lax.slice_in_dim(block, block.shape[dim] - width, None, axis...  120 us
    ppermute x4, waiting for transfers between devices, padded(): lax.ppermute(lax.slice_in_dim(block, 0, width, axis=dim), axis, backward)  119 us
    dot_general x52, matrix products, truncated(): jnp.einsum('xyij,xyjk->xyik', left[:, :, first], partner, preferred_eleme...  13.4 us
    ppermute x4, starting transfers between devices, padded(): lax.ppermute(lax.slice_in_dim(block, 0, width, axis=dim), axis, backward)  7.59 us
    all_gather x2, local copies, waits for them, and re-layouts, on_device(): joined = lax.all_gather(current, 'layer', axis=3, tiled=True)  7.26 us
    all_gather x2, blocking collectives, on_device(): joined = lax.all_gather(current, 'layer', axis=3, tiled=True)  6.65 us
  transfers between devices with their start and end apart: 8, of which 8 were waited for; matrix products, arithmetic and copies ran while one was open for 1% of the time, Pallas kernels for 0%

commit v1 on v0

v1 whole, which is shorter than its diff:
```python
import functools

import jax
import jax.numpy as jnp
from jax import lax
from jax.experimental import pallas as pl
from jax.experimental.pallas import tpu as pltpu
from jax.sharding import PartitionSpec as P

STEPS = 2
SLOTS = 5
OPPOSITE = (0, 2, 1, 4, 3)
MESH = pl.DeviceIdType.MESH


def edges_of(count):
    edges = [(a, j, j) for j in range(count) for a in (1, 2)]
    return edges + [(3, count - 1, 0), (4, 0, count - 1)]


def dot(left, right):
    return jnp.dot(left, right, preferred_element_type=jnp.float32)


def kernel(
    keep, density, out, full, pack, halo, acc, square,
    send_l, recv_l, send_h, recv_h, send_r, recv_r,
):
    count, _, rows, columns = density.shape
    high, wide = full.shape[-2:]
    main = wide // 128 * 128
    edges = edges_of(count)
    me = lax.axis_index("layer")
    x, y = lax.axis_index("gx"), lax.axis_index("gy")
    size_x, size_y = lax.axis_size("gx"), lax.axis_size("gy")
    partner = {"layer": 1 - me}
    towards = {
        1: {"gx": lax.rem(x + 1, size_x)},
        2: {"gx": lax.rem(x + size_x - 1, size_x)},
        3: {"gy": lax.rem(y + 1, size_y)},
        4: {"gy": lax.rem(y + size_y - 1, size_y)},
    }

    def local_copy(step, j):
        return pltpu.make_async_remote_copy(
            src_ref=full.at[step, j, :, me], dst_ref=full.at[step, j, :, me],
            send_sem=send_l.at[step, j], recv_sem=recv_l.at[step, j],
            device_id=partner, device_id_type=MESH,
        )

    def halo_copy(step, e):
        return pltpu.make_async_remote_copy(
            src_ref=pack.at[step, e], dst_ref=halo.at[step, e, me],
            send_sem=send_h.at[step, e], recv_sem=recv_h.at[step, e],
            device_id=towards[OPPOSITE[edges[e][0]]], device_id_type=MESH,
        )

    def relay_copy(step, e):
        return pltpu.make_async_remote_copy(
            src_ref=halo.at[step, e, me], dst_ref=halo.at[step, e, me],
            send_sem=send_r.at[step, e], recv_sem=recv_r.at[step, e],
            device_id=partner, device_id_type=MESH,
        )

    def mask(j, s):
        return keep[j * SLOTS + s].astype(jnp.float32)

    def send(step, j, blocks):
        for e, (a, _, source) in enumerate(edges):
            if source == j:
                own, other = blocks[0], blocks[OPPOSITE[a]]
                pack[step, e] = jnp.concatenate(
                    [own[:, :main], other[:, :main], own[:, main:], other[:, main:]], axis=-1
                ).astype(jnp.bfloat16)
                halo_copy(step, e).start()
        for s in range(SLOTS):
            full[step, j, s, me] = blocks[s].astype(jnp.bfloat16)
        local_copy(step, j).start()

    def whole(step, j, s):
        return full[step, j, s].reshape(2 * high, wide)

    def local_terms(step, j, block):
        own = block(0)
        sums = [dot(own, whole(step, j, s)) for s in range(SLOTS)]
        for a, other in ((3, j + 1), (4, j - 1)):
            if 0 <= other < count:
                left = block(a)
                sums[0] = sums[0] + dot(left, whole(step, other, OPPOSITE[a]))
                sums[a] = sums[a] + dot(left, whole(step, other, 0))
        return sums

    def halo_terms(step, j, block, sums):
        for e, (a, user, _) in enumerate(edges):
            if user == j:
                both = dot(block(a), halo[step, e].reshape(2 * high, 2 * wide))
                rest = 2 * main + wide - main
                sums[a] = sums[a] + jnp.concatenate([both[:, :main], both[:, 2 * main : rest]], axis=-1)
                sums[0] = sums[0] + jnp.concatenate([both[:, main : 2 * main], both[:, rest:]], axis=-1)
        return sums

    barrier = pltpu.get_barrier_semaphore()
    for device in (partner, *towards.values()):
        pl.semaphore_signal(barrier, inc=1, device_id=device, device_id_type=MESH)
    pl.semaphore_wait(barrier, 5)

    row = lax.broadcasted_iota(jnp.int32, (columns, wide), 0)
    column = lax.broadcasted_iota(jnp.int32, (columns, wide), 1)
    spread = jnp.where(row + jnp.where(row >= rows, high - rows, 0) == column, 1.0, 0.0).astype(jnp.bfloat16)
    row = lax.broadcasted_iota(jnp.int32, (wide, columns), 0)
    column = lax.broadcasted_iota(jnp.int32, (wide, columns), 1)
    gather = jnp.where(column + jnp.where(column >= rows, high - rows, 0) == row, 1.0, 0.0).astype(jnp.bfloat16)

    for j in range(count):
        blocks = []
        for s in range(SLOTS):
            block = (density[j, s].astype(jnp.float32) * mask(j, s)).astype(jnp.bfloat16)
            block = dot(block, spread)
            blocks.append(jnp.concatenate([block, jnp.zeros((high - rows, wide), jnp.float32)], axis=0))
        send(0, j, blocks)

    for step in range(STEPS):
        for j in range(count):
            local_copy(step, j).wait_recv()
        for j in range(count):
            sums = local_terms(step, j, lambda a: full[step, j, a, me])
            for s in range(SLOTS):
                acc[j, s] = sums[s]
        for j in range(count):
            mine = [e for e in range(len(edges)) if edges[e][1] == j]
            for e in mine:
                halo_copy(step, e).wait_recv()
                relay_copy(step, e).start()
            for e in mine:
                relay_copy(step, e).wait_recv()
            sums = [acc[j, s] for s in range(SLOTS)]
            sums = halo_terms(step, j, lambda a: full[step, j, a, me], sums)
            for s in range(SLOTS):
                square[j, s] = (sums[s] * mask(j, s)).astype(jnp.bfloat16)
            sums = local_terms(step, j, lambda a: square[j, a])
            sums = halo_terms(step, j, lambda a: square[j, a], sums)
            blocks = []
            for s in range(SLOTS):
                cube = (sums[s] * mask(j, s)).astype(jnp.bfloat16).astype(jnp.float32)
                blocks.append(3.0 * square[j, s].astype(jnp.float32) - 2.0 * cube)
            if step < STEPS - 1:
                send(step + 1, j, blocks)
            else:
                for s in range(SLOTS):
                    block = dot(blocks[s].astype(jnp.bfloat16), gather)
                    out[j, s] = block[:rows].astype(jnp.bfloat16)

    for step in range(STEPS):
        for j in range(count):
            local_copy(step, j).wait_send()
        for e in range(len(edges)):
            halo_copy(step, e).wait_send()
            relay_copy(step, e).wait_send()


def on_device(density, pattern):
    _, count, slots, rows, columns = density.shape
    high = -(-rows // 16) * 16
    wide = 2 * high
    number = len(edges_of(count))
    dma = pltpu.SemaphoreType.DMA
    out = pl.pallas_call(
        kernel,
        out_shape=jax.ShapeDtypeStruct((count, slots, rows, columns), jnp.bfloat16),
        in_specs=[pl.BlockSpec(memory_space=pltpu.SMEM), pl.BlockSpec(memory_space=pltpu.VMEM)],
        out_specs=pl.BlockSpec(memory_space=pltpu.VMEM),
        scratch_shapes=[
            pltpu.VMEM((STEPS, count, slots, 2, high, wide), jnp.bfloat16),
            pltpu.VMEM((STEPS, number, high, 2 * wide), jnp.bfloat16),
            pltpu.VMEM((STEPS, number, 2, high, 2 * wide), jnp.bfloat16),
            pltpu.VMEM((count, slots, high, wide), jnp.float32),
            pltpu.VMEM((count, slots, high, wide), jnp.bfloat16),
            dma((STEPS, count)), dma((STEPS, count)),
            dma((STEPS, number)), dma((STEPS, number)),
            dma((STEPS, number)), dma((STEPS, number)),
        ],
        compiler_params=pltpu.CompilerParams(
            collective_id=0, has_side_effects=True, vmem_limit_bytes=40 * 1024 * 1024
        ),
    )(pattern.reshape(-1), density[0])
    return out[None]


def solution(mesh):
    return jax.shard_map(
        on_device,
        mesh=mesh,
        in_specs=(P(("groups", "gx"), "gy", None, "layer", None), P(("groups", "gx"), "gy", None)),
        out_specs=P(("groups", "gx"), "gy", None, "layer", None),
        check_vma=False,
    )
```

time: 290 us -> 33.2 us (0.11)
  waiting for transfers between devices: 239 us -> 0 us
  Pallas kernels: 0 us -> 29.5 us
  matrix products: 13.4 us -> 0 us
  starting transfers between devices: 11.2 us -> 0 us
  local copies, waits for them, and re-layouts: 11.5 us -> 2.81 us
  other arithmetic: 7.71 us -> 0.7 us
  blocking collectives: 6.65 us -> 0 us
    ppermute x8 -> x0, waiting for transfers between devices: 239 us -> none  [the longest x4 120 us: padded(): lax.ppermute(lax.slice_in_dim(block, block.shape[dim] - width, None, axis...]
    pallas_call x0 -> x1, Pallas kernels: none -> 29.5 us  [on_device(): pl.pallas_call(kernel, out_shape=jax.ShapeDtypeStruct((count, slots, rows...]
    dot_general x52 -> x0, matrix products: 13.4 us -> none  [truncated(): jnp.einsum('xyij,xyjk->xyik', left[:, :, first], partner, preferred_eleme...]
    ppermute x8 -> x0, starting transfers between devices: 11.2 us -> none  [the longest x4 7.59 us: padded(): lax.ppermute(lax.slice_in_dim(block, 0, width, axis=dim), axis, backward)]
    all_gather x2 -> x0, local copies, waits for them, and re-layouts: 7.26 us -> none  [on_device(): joined = lax.all_gather(current, 'layer', axis=3, tiled=True)]
    all_gather x2 -> x0, blocking collectives: 6.65 us -> none  [on_device(): joined = lax.all_gather(current, 'layer', axis=3, tiled=True)]
  transfers between devices with their start and end apart: 8 -> 0, of which waited for: 8 -> 0; matrix products, arithmetic and copies ran while one was open for 1% -> 0% of each run, Pallas kernels for 0% -> 0%
where the time goes in v1:
time: 33.2 us; the launch traced here: 33 us
  Pallas kernels  29.5 us (89%)
  local copies, waits for them, and re-layouts  2.81 us (8%)
  other arithmetic  0.7 us (2%)
    pallas_call x1, Pallas kernels, on_device(): pl.pallas_call(kernel, out_shape=jax.ShapeDtypeStruct((count, slots, rows...  29.5 us
    unnamed x1, local copies, waits for them, and re-layouts  1.51 us
    broadcast_in_dim x1, local copies, waits for them, and re-layouts, on_device(): return out[None]  1.22 us
    unnamed x1, other arithmetic  0.7 us

profile of v1, /device:TPU:0, one launch (start us, length us, event | category | flops | bytes accessed | tf_op | source)
XLA Modules:
  0.0 33.0 jit_solution(16175650320530082885)
XLA Ops:
  0.0 0.7 %reduce = s32[3,5]{1,0:T(4,128)S(1)} reduce(s32[1,3,5]{2,0,1:T(1,128)} %param.3, s32[]{:T(128)} %constant.2), dimensions={0}, to_apply=%param.3.reduce_sub_computation | reduce | bytes 124 | tf_op args[1]
  0.7 0.1 reshape.3.keep
  0.8 1.5 %copy.3 = bf16[1,3,5,92,184]{4,3,2,1,0:T(8,128)(2,1)S(1)} copy(bf16[1,3,5,92,184]{3,4,2,1,0:T(8,128)(2,1)} %param.2) | data formatting | bytes 1015680 | tf_op args[0]
  2.3 29.5 %shard_map.28 = bf16[3,5,92,184]{3,2,1,0:T(8,128)(2,1)S(1)} custom-call(s32[15]{0:T(128)S(1)} %reshape.3.keep, bf16[3,5,92,184]{3,2,1,0:T(8,128)(2,1)S(1)} %bitcast.3), custom_call_target="tpu_custom_call" | custom-call | tf_op jit(solution)/shard_map/pallas_call | solution.py:167
  31.8 1.2 %copy.4 = bf16[1,3,5,92,184]{3,4,2,1,0:T(8,128)(2,1)} copy(bf16[1,3,5,92,184]{4,3,2,1,0:T(8,128)(2,1)S(1)} %bitcast.2) | data formatting | bytes 1015680 | tf_op jit(solution)/shard_map/broadcast_in_dim | solution.py:186

commit v2 on v1

--- a/solution.py
+++ b/solution.py
@@ -18,15 +18,17 @@
     return edges + [(3, count - 1, 0), (4, 0, count - 1)]
 
 
-def dot(left, right):
-    return jnp.dot(left, right, preferred_element_type=jnp.float32)
+def dot(left, right, first=1, second=0):
+    return lax.dot_general(
+        left, right, (((first,), (second,)), ((), ())), preferred_element_type=jnp.float32
+    )
 
 
 def kernel(
     keep, density, out, full, pack, halo, acc, square,
     send_l, recv_l, send_h, recv_h, send_r, recv_r,
 ):
-    count, _, rows, columns = density.shape
+    count, _, columns, rows = density.shape
     high, wide = full.shape[-2:]
     main = wide // 128 * 128
     edges = edges_of(count)
@@ -63,7 +65,7 @@
         )
 
     def mask(j, s):
-        return keep[j * SLOTS + s].astype(jnp.float32)
+        return keep[j, 0, s].astype(jnp.float32)
 
     def send(step, j, blocks):
         for e, (a, _, source) in enumerate(edges):
@@ -107,15 +109,12 @@
     row = lax.broadcasted_iota(jnp.int32, (columns, wide), 0)
     column = lax.broadcasted_iota(jnp.int32, (columns, wide), 1)
     spread = jnp.where(row + jnp.where(row >= rows, high - rows, 0) == column, 1.0, 0.0).astype(jnp.bfloat16)
-    row = lax.broadcasted_iota(jnp.int32, (wide, columns), 0)
-    column = lax.broadcasted_iota(jnp.int32, (wide, columns), 1)
-    gather = jnp.where(column + jnp.where(column >= rows, high - rows, 0) == row, 1.0, 0.0).astype(jnp.bfloat16)
 
     for j in range(count):
         blocks = []
         for s in range(SLOTS):
             block = (density[j, s].astype(jnp.float32) * mask(j, s)).astype(jnp.bfloat16)
-            block = dot(block, spread)
+            block = dot(block, spread, 0, 0)
             blocks.append(jnp.concatenate([block, jnp.zeros((high - rows, wide), jnp.float32)], axis=0))
         send(0, j, blocks)
 
@@ -147,8 +146,8 @@
                 send(step + 1, j, blocks)
             else:
                 for s in range(SLOTS):
-                    block = dot(blocks[s].astype(jnp.bfloat16), gather)
-                    out[j, s] = block[:rows].astype(jnp.bfloat16)
+                    block = dot(spread, blocks[s].astype(jnp.bfloat16), 1, 1)
+                    out[j, s] = block[:, :rows].astype(jnp.bfloat16)
 
     for step in range(STEPS):
         for j in range(count):
@@ -166,7 +165,7 @@
     dma = pltpu.SemaphoreType.DMA
     out = pl.pallas_call(
         kernel,
-        out_shape=jax.ShapeDtypeStruct((count, slots, rows, columns), jnp.bfloat16),
+        out_shape=jax.ShapeDtypeStruct((count, slots, columns, rows), jnp.bfloat16),
         in_specs=[pl.BlockSpec(memory_space=pltpu.SMEM), pl.BlockSpec(memory_space=pltpu.VMEM)],
         out_specs=pl.BlockSpec(memory_space=pltpu.VMEM),
         scratch_shapes=[
@@ -182,8 +181,8 @@
         compiler_params=pltpu.CompilerParams(
             collective_id=0, has_side_effects=True, vmem_limit_bytes=40 * 1024 * 1024
         ),
-    )(pattern.reshape(-1), density[0])
-    return out[None]
+    )(jnp.swapaxes(pattern, 0, 1), jnp.swapaxes(density[0], 2, 3))
+    return jnp.swapaxes(out, 2, 3)[None]
 
 
 def solution(mesh):

time: 33.2 us -> 32.6 us (0.982)
  other arithmetic: 0.7 us -> 0 us
    broadcast_in_dim x1 -> x0, local copies, waits for them, and re-layouts: 1.22 us -> none  [on_device(): return out[None]]
    unnamed x1 -> x5, local copies, waits for them, and re-layouts: 1.51 us -> 2.64 us
    unnamed x1 -> x0, other arithmetic: 0.7 us -> none
where the time goes in v2:
time: 32.6 us; the launch traced here: 32.4 us
  Pallas kernels  29.8 us (91%)
  local copies, waits for them, and re-layouts  2.64 us (8%)
    pallas_call x1, Pallas kernels, on_device(): pl.pallas_call(kernel, out_shape=jax.ShapeDtypeStruct((count, slots, colu...  29.8 us
    unnamed x5, local copies, waits for them, and re-layouts  2.64 us

profile of v2, /device:TPU:0, one launch (start us, length us, event | category | flops | bytes accessed | tf_op | source)
XLA Modules:
  0.0 32.4 jit_solution(7994627228778142896)
XLA Ops:
  0.0 0.0 copy-start.1
  0.0 0.7 %copy-done.1 = s32[1,3,5]{2,0,1:T(1,128)S(1)} copy-done((s32[1,3,5]{2,0,1:T(1,128)S(1)}, s32[1,3,5]{2,0,1:T(1,128)}, u32[]{:S(2)}) %copy-start.1) | copy-done | bytes 84
  0.7 0.0 copy-start
  0.7 1.1 %copy-done = bf16[1,3,5,92,184]{3,4,2,1,0:T(8,128)(2,1)S(1)} copy-done((bf16[1,3,5,92,184]{3,4,2,1,0:T(8,128)(2,1)S(1)}, bf16[1,3,5,92,184]{3,4,2,1,0:T(8,128)(2,1)}, u32[]{:S(2)}) %copy-start) | copy-done | bytes 507864
  1.8 29.8 %shard_map.28 = bf16[3,5,184,92]{3,2,1,0:T(8,128)(2,1)S(1)} custom-call(s32[3,1,5]{2,1,0:T(1,128)S(1)} %bitcast.9, bf16[3,5,184,92]{3,2,1,0:T(8,128)(2,1)S(1)} %bitcast.8), custom_call_target="tpu_custom_call" | custom-call | tf_op jit(solution)/shard_map/pallas_call | solution.py:166
  31.6 0.9 %copy.4 = bf16[1,3,5,92,184]{3,4,2,1,0:T(8,128)(2,1)} copy(bf16[1,3,5,92,184]{3,4,2,1,0:T(8,128)(2,1)S(1)} %bitcast.7) | data formatting | bytes 1015680
Async XLA Ops:
  0.0 0.7 %copy-start.1 = (s32[1,3,5]{2,0,1:T(1,128)S(1)}, s32[1,3,5]{2,0,1:T(1,128)}, u32[]{:S(2)}) copy-start(s32[1,3,5]{2,0,1:T(1,128)} %param.3) | copy-start | bytes 184
  0.7 1.1 %copy-start = (bf16[1,3,5,92,184]{3,4,2,1,0:T(8,128)(2,1)S(1)}, bf16[1,3,5,92,184]{3,4,2,1,0:T(8,128)(2,1)}, u32[]{:S(2)}) copy-start(bf16[1,3,5,92,184]{3,4,2,1,0:T(8,128)(2,1)} %param.2) | copy-start | bytes 1523524

commit v3 on v2

--- a/solution.py
+++ b/solution.py
@@ -25,8 +25,8 @@
 
 
 def kernel(
-    keep, density, out, full, pack, halo, acc, square,
-    send_l, recv_l, send_h, recv_h, send_r, recv_r,
+    pattern, density, out, full, pack, halo, acc, square, keep, staged,
+    send_l, recv_l, send_h, recv_h, send_r, recv_r, load, load_keep,
 ):
     count, _, columns, rows = density.shape
     high, wide = full.shape[-2:]
@@ -67,17 +67,18 @@
     def mask(j, s):
         return keep[j, 0, s].astype(jnp.float32)
 
-    def send(step, j, blocks):
+    def send_halo(step, j, blocks, slots):
         for e, (a, _, source) in enumerate(edges):
-            if source == j:
+            if source == j and a in slots:
                 own, other = blocks[0], blocks[OPPOSITE[a]]
                 pack[step, e] = jnp.concatenate(
                     [own[:, :main], other[:, :main], own[:, main:], other[:, main:]], axis=-1
                 ).astype(jnp.bfloat16)
                 halo_copy(step, e).start()
-        for s in range(SLOTS):
+
+    def store(step, j, blocks, slots):
+        for s in slots:
             full[step, j, s, me] = blocks[s].astype(jnp.bfloat16)
-        local_copy(step, j).start()
 
     def whole(step, j, s):
         return full[step, j, s].reshape(2 * high, wide)
@@ -104,19 +105,35 @@
     barrier = pltpu.get_barrier_semaphore()
     for device in (partner, *towards.values()):
         pl.semaphore_signal(barrier, inc=1, device_id=device, device_id_type=MESH)
-    pl.semaphore_wait(barrier, 5)
+    loads = [pltpu.make_async_copy(density.at[j], staged.at[j], load.at[j]) for j in range(count)]
+    load_pattern = pltpu.make_async_copy(pattern, keep, load_keep)
+    load_pattern.start()
+    for copy in loads:
+        copy.start()
 
     row = lax.broadcasted_iota(jnp.int32, (columns, wide), 0)
     column = lax.broadcasted_iota(jnp.int32, (columns, wide), 1)
     spread = jnp.where(row + jnp.where(row >= rows, high - rows, 0) == column, 1.0, 0.0).astype(jnp.bfloat16)
 
+    load_pattern.wait()
+
+    def begin(j, s):
+        block = (staged[j, s].astype(jnp.float32) * mask(j, s)).astype(jnp.bfloat16)
+        block = dot(block, spread, 0, 0)
+        return jnp.concatenate([block, jnp.zeros((high - rows, wide), jnp.float32)], axis=0)
+
     for j in range(count):
-        blocks = []
-        for s in range(SLOTS):
-            block = (density[j, s].astype(jnp.float32) * mask(j, s)).astype(jnp.bfloat16)
-            block = dot(block, spread, 0, 0)
-            blocks.append(jnp.concatenate([block, jnp.zeros((high - rows, wide), jnp.float32)], axis=0))
-        send(0, j, blocks)
+        loads[j].wait()
+        blocks = [begin(j, s) for s in range(3)]
+        if j == 0:
+            pl.semaphore_wait(barrier, 5)
+        send_halo(0, j, blocks, (1, 2))
+        store(0, j, blocks, range(3))
+    for j in range(count):
+        blocks = [begin(j, s) if s % 3 == 0 or s == 4 else None for s in range(SLOTS)]
+        send_halo(0, j, blocks, (3, 4))
+        store(0, j, blocks, (3, 4))
+        local_copy(0, j).start()
 
     for step in range(STEPS):
         for j in range(count):
@@ -143,7 +160,9 @@
                 cube = (sums[s] * mask(j, s)).astype(jnp.bfloat16).astype(jnp.float32)
                 blocks.append(3.0 * square[j, s].astype(jnp.float32) - 2.0 * cube)
             if step < STEPS - 1:
-                send(step + 1, j, blocks)
+                send_halo(step + 1, j, blocks, (1, 2, 3, 4))
+                store(step + 1, j, blocks, range(SLOTS))
+                local_copy(step + 1, j).start()
             else:
                 for s in range(SLOTS):
                     block = dot(spread, blocks[s].astype(jnp.bfloat16), 1, 1)
@@ -165,8 +184,8 @@
     dma = pltpu.SemaphoreType.DMA
     out = pl.pallas_call(
         kernel,
-        out_shape=jax.ShapeDtypeStruct((count, slots, columns, rows), jnp.bfloat16),
-        in_specs=[pl.BlockSpec(memory_space=pltpu.SMEM), pl.BlockSpec(memory_space=pltpu.VMEM)],
+        out_shape=pltpu.VMEM((count, slots, columns, rows), jnp.bfloat16),
+        in_specs=[pl.BlockSpec(memory_space=pltpu.HBM)] * 2,
         out_specs=pl.BlockSpec(memory_space=pltpu.VMEM),
         scratch_shapes=[
             pltpu.VMEM((STEPS, count, slots, 2, high, wide), jnp.bfloat16),
@@ -174,12 +193,15 @@
             pltpu.VMEM((STEPS, number, 2, high, 2 * wide), jnp.bfloat16),
             pltpu.VMEM((count, slots, high, wide), jnp.float32),
             pltpu.VMEM((count, slots, high, wide), jnp.bfloat16),
+            pltpu.SMEM((count, 1, slots), jnp.int32),
+            pltpu.VMEM((count, slots, columns, rows), jnp.bfloat16),
             dma((STEPS, count)), dma((STEPS, count)),
             dma((STEPS, number)), dma((STEPS, number)),
             dma((STEPS, number)), dma((STEPS, number)),
+            dma((count,)), dma,
         ],
         compiler_params=pltpu.CompilerParams(
-            collective_id=0, has_side_effects=True, vmem_limit_bytes=40 * 1024 * 1024
+            collective_id=0, has_side_effects=True, vmem_limit_bytes=60 * 1024 * 1024
         ),
     )(jnp.swapaxes(pattern, 0, 1), jnp.swapaxes(density[0], 2, 3))
     return jnp.swapaxes(out, 2, 3)[None]

time: 32.6 us -> 30.4 us (0.933)
  local copies, waits for them, and re-layouts: 2.64 us -> 0.86 us
  Pallas kernels: 29.8 us -> 29.4 us
    unnamed x5 -> x1, local copies, waits for them, and re-layouts: 2.64 us -> 0.86 us
where the time goes in v3:
time: 30.4 us; the launch traced here: 30.3 us
  Pallas kernels  29.4 us (97%)
  local copies, waits for them, and re-layouts  0.86 us (3%)
    pallas_call x1, Pallas kernels, on_device(): pl.pallas_call(kernel, out_shape=pltpu.VMEM((count, slots, columns, rows)...  29.4 us
    unnamed x1, local copies, waits for them, and re-layouts  0.86 us

profile of v3, /device:TPU:0, one launch (start us, length us, event | category | flops | bytes accessed | tf_op | source)
XLA Modules:
  0.0 30.3 jit_solution(16329926115385646454)
XLA Ops:
  0.0 29.4 %shard_map.28 = bf16[3,5,184,92]{3,2,1,0:T(8,128)(2,1)S(1)} custom-call(s32[3,1,5]{2,1,0:T(1,128)} %bitcast.9, bf16[3,5,184,92]{3,2,1,0:T(8,128)(2,1)} %bitcast.8), custom_call_target="tpu_custom_call" | custom-call | tf_op jit(solution)/shard_map/pallas_call | solution.py:185
  29.4 0.9 %copy.4 = bf16[1,3,5,92,184]{3,4,2,1,0:T(8,128)(2,1)} copy(bf16[1,3,5,92,184]{3,4,2,1,0:T(8,128)(2,1)S(1)} %bitcast.7) | data formatting | bytes 1015680

commit v4 on v3

--- a/solution.py
+++ b/solution.py
@@ -67,14 +67,23 @@
     def mask(j, s):
         return keep[j, 0, s].astype(jnp.float32)
 
-    def send_halo(step, j, blocks, slots):
+    def pack_halo(step, j, blocks, slots):
         for e, (a, _, source) in enumerate(edges):
             if source == j and a in slots:
                 own, other = blocks[0], blocks[OPPOSITE[a]]
                 pack[step, e] = jnp.concatenate(
                     [own[:, :main], other[:, :main], own[:, main:], other[:, main:]], axis=-1
                 ).astype(jnp.bfloat16)
-                halo_copy(step, e).start()
+
+    def send_halo(step, j, slots):
+        for a in slots:
+            for e, edge in enumerate(edges):
+                if edge[0] == a and edge[2] == j:
+                    halo_copy(step, e).start()
+
+    def send_x(step, j):
+        pl.when(x == size_x - 1)(lambda: send_halo(step, j, (2, 1)))
+        pl.when(x != size_x - 1)(lambda: send_halo(step, j, (1, 2)))
 
     def store(step, j, blocks, slots):
         for s in slots:
@@ -125,13 +134,15 @@
     for j in range(count):
         loads[j].wait()
         blocks = [begin(j, s) for s in range(3)]
+        pack_halo(0, j, blocks, (1, 2))
         if j == 0:
             pl.semaphore_wait(barrier, 5)
-        send_halo(0, j, blocks, (1, 2))
+        send_x(0, j)
         store(0, j, blocks, range(3))
     for j in range(count):
         blocks = [begin(j, s) if s % 3 == 0 or s == 4 else None for s in range(SLOTS)]
-        send_halo(0, j, blocks, (3, 4))
+        pack_halo(0, j, blocks, (3, 4))
+        send_halo(0, j, (3, 4))
         store(0, j, blocks, (3, 4))
         local_copy(0, j).start()
 
@@ -160,7 +171,9 @@
                 cube = (sums[s] * mask(j, s)).astype(jnp.bfloat16).astype(jnp.float32)
                 blocks.append(3.0 * square[j, s].astype(jnp.float32) - 2.0 * cube)
             if step < STEPS - 1:
-                send_halo(step + 1, j, blocks, (1, 2, 3, 4))
+                pack_halo(step + 1, j, blocks, (1, 2, 3, 4))
+                send_x(step + 1, j)
+                send_halo(step + 1, j, (3, 4))
                 store(step + 1, j, blocks, range(SLOTS))
                 local_copy(step + 1, j).start()
             else:

time: 30.4 us -> 28.9 us (0.951)
  Pallas kernels: 29.4 us -> 27.9 us
    pallas_call x1, Pallas kernels: 29.4 us -> 27.9 us  [on_device(): pl.pallas_call(kernel, out_shape=pltpu.VMEM((count, slots, columns, rows)...]
where the time goes in v4:
time: 28.9 us; the launch traced here: 28.7 us
  Pallas kernels  27.9 us (97%)
  local copies, waits for them, and re-layouts  0.86 us (3%)
    pallas_call x1, Pallas kernels, on_device(): pl.pallas_call(kernel, out_shape=pltpu.VMEM((count, slots, columns, rows)...  27.9 us
    unnamed x1, local copies, waits for them, and re-layouts  0.86 us

profile of v4, /device:TPU:0, one launch (start us, length us, event | category | flops | bytes accessed | tf_op | source)
XLA Modules:
  0.0 28.7 jit_solution(5470624665730991238)
XLA Ops:
  0.0 27.9 %shard_map.28 = bf16[3,5,184,92]{3,2,1,0:T(8,128)(2,1)S(1)} custom-call(s32[3,1,5]{2,1,0:T(1,128)} %bitcast.9, bf16[3,5,184,92]{3,2,1,0:T(8,128)(2,1)} %bitcast.8), custom_call_target="tpu_custom_call" | custom-call | tf_op jit(solution)/shard_map/pallas_call | solution.py:198
  27.9 0.9 %copy.4 = bf16[1,3,5,92,184]{3,4,2,1,0:T(8,128)(2,1)} copy(bf16[1,3,5,92,184]{3,4,2,1,0:T(8,128)(2,1)S(1)} %bitcast.7) | data formatting | bytes 1015680

commit v5 on v4

--- a/solution.py
+++ b/solution.py
@@ -32,6 +32,7 @@
     high, wide = full.shape[-2:]
     main = wide // 128 * 128
     edges = edges_of(count)
+    order = (0, *range(count - 1, 0, -1))
     me = lax.axis_index("layer")
     x, y = lax.axis_index("gx"), lax.axis_index("gy")
     size_x, size_y = lax.axis_size("gx"), lax.axis_size("gy")
@@ -114,11 +115,17 @@
     barrier = pltpu.get_barrier_semaphore()
     for device in (partner, *towards.values()):
         pl.semaphore_signal(barrier, inc=1, device_id=device, device_id_type=MESH)
-    loads = [pltpu.make_async_copy(density.at[j], staged.at[j], load.at[j]) for j in range(count)]
+    parts = [(j, p) for p in range(2) for j in order]
+    loads = {
+        (j, p): pltpu.make_async_copy(
+            density.at[j, pl.ds(3 * p, 3 - p)], staged.at[j, pl.ds(3 * p, 3 - p)], load.at[j, p]
+        )
+        for j, p in parts
+    }
     load_pattern = pltpu.make_async_copy(pattern, keep, load_keep)
     load_pattern.start()
-    for copy in loads:
-        copy.start()
+    for part in parts:
+        loads[part].start()
 
     row = lax.broadcasted_iota(jnp.int32, (columns, wide), 0)
     column = lax.broadcasted_iota(jnp.int32, (columns, wide), 1)
@@ -131,15 +138,16 @@
         block = dot(block, spread, 0, 0)
         return jnp.concatenate([block, jnp.zeros((high - rows, wide), jnp.float32)], axis=0)
 
-    for j in range(count):
-        loads[j].wait()
+    for j in order:
+        loads[j, 0].wait()
         blocks = [begin(j, s) for s in range(3)]
         pack_halo(0, j, blocks, (1, 2))
         if j == 0:
             pl.semaphore_wait(barrier, 5)
         send_x(0, j)
         store(0, j, blocks, range(3))
-    for j in range(count):
+    for j in order:
+        loads[j, 1].wait()
         blocks = [begin(j, s) if s % 3 == 0 or s == 4 else None for s in range(SLOTS)]
         pack_halo(0, j, blocks, (3, 4))
         send_halo(0, j, (3, 4))
@@ -153,7 +161,7 @@
             sums = local_terms(step, j, lambda a: full[step, j, a, me])
             for s in range(SLOTS):
                 acc[j, s] = sums[s]
-        for j in range(count):
+        for j in order:
             mine = [e for e in range(len(edges)) if edges[e][1] == j]
             for e in mine:
                 halo_copy(step, e).wait_recv()
@@ -211,7 +219,7 @@
             dma((STEPS, count)), dma((STEPS, count)),
             dma((STEPS, number)), dma((STEPS, number)),
             dma((STEPS, number)), dma((STEPS, number)),
-            dma((count,)), dma,
+            dma((count, 2)), dma,
         ],
         compiler_params=pltpu.CompilerParams(
             collective_id=0, has_side_effects=True, vmem_limit_bytes=60 * 1024 * 1024

time: 28.9 us -> 28.7 us (level)
  the two profiles are of different devices: /device:TPU:0 before, /device:TPU:1 now
where the time goes in v5:
time: 28.7 us; the launch traced here: 28.5 us
  Pallas kernels  27.7 us (97%)
  local copies, waits for them, and re-layouts  0.86 us (3%)
    pallas_call x1, Pallas kernels, on_device(): pl.pallas_call(kernel, out_shape=pltpu.VMEM((count, slots, columns, rows)...  27.7 us
    unnamed x1, local copies, waits for them, and re-layouts  0.86 us

profile of v5, /device:TPU:1, one launch (start us, length us, event | category | flops | bytes accessed | tf_op | source)
XLA Modules:
  0.0 28.5 jit_solution(6642500793951852498)
XLA Ops:
  0.0 27.7 %shard_map.28 = bf16[3,5,184,92]{3,2,1,0:T(8,128)(2,1)S(1)} custom-call(s32[3,1,5]{2,1,0:T(1,128)} %bitcast.9, bf16[3,5,184,92]{3,2,1,0:T(8,128)(2,1)} %bitcast.8), custom_call_target="tpu_custom_call" | custom-call | tf_op jit(solution)/shard_map/pallas_call | solution.py:206
  27.7 0.9 %copy.4 = bf16[1,3,5,92,184]{3,4,2,1,0:T(8,128)(2,1)} copy(bf16[1,3,5,92,184]{3,4,2,1,0:T(8,128)(2,1)S(1)} %bitcast.7) | data formatting | bytes 1015680
